TPU v7x, 128 devices: a whole 4x4x4 slice. The times are simulated.
128 devices in a mesh: dp: 8 (over y, core), vocab: 16 (over x, z).
Axes of the slice: x: 4, y: 4, z: 4, core: 2. Of those that a mesh axis runs over, the one named last changes fastest.
Arguments:
- hidden: bfloat16 [512, 3072], P(('dp', 'vocab')), may hold values from -16 to 16
- head_weight: bfloat16 [3072, 128256], P(None, ('dp', 'vocab')), may hold values from -1 to 1
- teacher: bfloat16 [512, 128256], P(('dp', 'vocab')), may hold values from -300 to 300
- row_token: int32 [512], replicated, may hold values from 0 to 511, each once
- labels: int32 [512], replicated, may hold values from 0 to 128255
Outputs:
- hidden_grad: float32 [512, 3072], P(('dp', 'vocab'))
- head_grad: float32 [3072, 128256], P(None, ('dp', 'vocab'))
- distill_loss: float32 [], replicated
Inputs may be any that keep to these rules, and one draw needn't show every extreme that they name: row_token is a permutation of the 512 tokens.
All inputs are finite; a program needn't handle non-finite values.
Results may differ from a plain program's by a relative error of at most 0.0028.
Values may be sent and summed in bfloat16 or wider, within the bound.
No kernel may reach another device: no remote copies, remote signals or barrier semaphores. Data moves between devices by JAX's collectives and lax.ppermute only.
A program may use at most 128 MiB of HBM per device.

v0:
```python
import jax
import jax.numpy as jnp
from jax import lax
from jax.sharding import PartitionSpec as P


def per_device(hidden, head_weight, teacher, row_token, labels):
    shard_width = head_weight.shape[1]
    gathered = lax.all_gather(hidden, ("dp", "vocab"), axis=0, tiled=True)
    student = jnp.dot(gathered, head_weight, preferred_element_type=jnp.float32)
    row_total = gathered.shape[0]
    where_row = (
        jnp.zeros((row_total,), jnp.int32).at[row_token].set(jnp.arange(row_total, dtype=jnp.int32))
    )
    loaded = lax.all_to_all(teacher, ("dp", "vocab"), split_axis=1, concat_axis=0, tiled=True)
    taught = jnp.take(loaded, where_row, axis=0).astype(jnp.float32)
    offset = lax.axis_index(("dp", "vocab")) * shard_width
    columns = offset + lax.iota(jnp.int32, shard_width)
    label_hit = labels[:, None] == columns[None, :]
    picked_local = jnp.sum(jnp.where(label_hit, student, 0.0), axis=1)
    top_student = jnp.max(student, axis=1)
    top_teacher = jnp.max(taught, axis=1)
    top_student, top_teacher = lax.pmax((top_student, top_teacher), ("dp", "vocab"))
    exp_student = jnp.exp(student - top_student[:, None])
    exp_teacher = jnp.exp(taught - top_teacher[:, None])
    sum_student, sum_teacher, weighted, picked = lax.psum(
        (
            jnp.sum(exp_student, axis=1),
            jnp.sum(exp_teacher, axis=1),
            jnp.sum(exp_teacher * (taught - student), axis=1),
            picked_local,
        ),
        ("dp", "vocab"),
    )
    lse_student = top_student + jnp.log(sum_student)
    lse_teacher = top_teacher + jnp.log(sum_teacher)
    divergence = weighted / sum_teacher - lse_teacher + lse_student
    distill_loss = jnp.mean(divergence + 0.25 * (lse_student - picked))
    prob_student = exp_student / sum_student[:, None]
    prob_teacher = exp_teacher / sum_teacher[:, None]
    dlogits = (
        64.0 * (1.25 * prob_student - prob_teacher - 0.25 * label_hit.astype(jnp.float32))
    ).astype(jnp.bfloat16)
    head_grad = lax.dot_general(
        gathered, dlogits, (((0,), (0,)), ((), ())), preferred_element_type=jnp.float32
    )
    hidden_grad = lax.psum_scatter(
        lax.dot_general(
            dlogits, head_weight, (((1,), (1,)), ((), ())), preferred_element_type=jnp.float32
        ),
        ("dp", "vocab"),
        scatter_dimension=0,
        tiled=True,
    )
    return (hidden_grad, head_grad, distill_loss)


def solution(mesh):
    in_specs = (
        P(("dp", "vocab"), None),
        P(None, ("dp", "vocab")),
        P(("dp", "vocab"), None),
        P(),
        P(),
    )
    out_specs = (P(("dp", "vocab"), None), P(None, ("dp", "vocab")), P())
    return jax.shard_map(
        per_device, mesh=mesh, in_specs=in_specs, out_specs=out_specs, check_vma=False
    )
```

profile of v0, /device:TPU:1, one launch (start us, length us, event | category | flops | bytes accessed | tf_op | source)
XLA Modules:
  0.0 399.3 jit_solution(15184477542865391914)
XLA Ops:
  7.2 0.0 all-gather.3.cloned.1.call-start
  7.2 0.7 all-gather.3.cloned.1.call-update
  7.9 3.0 all_to_all.14
  10.9 0.0 copy-start
  10.9 1.8 copy.12
  12.7 11.5 %all-to-all-start = ((bf16[4,128,1002]{2,0,1:T(4,128)(2,1)}), bf16[4,128,1002]{2,0,1:T(4,128)(2,1)S(1)}, u32[]{:S(2)}, u32[]{:S(2)}) async-start(bf16[4,128,1002]{2,0,1:T(4,128)(2,1)} %copy.12), calls=%async_computation | async-start | bytes 2097152 | tf_op jit(solution)/shard_map/all_to_all | solution.py:15
  24.2 0.0 all-reduce.5.cloned.1.call-start
  24.2 0.0 copy-done
  24.3 2.4 scatter_custom_fusion
  26.8 16.2 %all-to-all-done = bf16[4,128,1002]{2,0,1:T(4,128)(2,1)S(1)} async-done(((bf16[4,128,1002]{2,0,1:T(4,128)(2,1)}), bf16[4,128,1002]{2,0,1:T(4,128)(2,1)S(1)}, u32[]{:S(2)}, u32[]{:S(2)}) %all-to-all-start) | async-done | bytes 1026080 | tf_op jit(solution)/shard_map/all_to_all | solution.py:15
  43.0 0.5 all_to_all.17
  43.5 2.1 gather_fusion
  45.6 0.5 copy.13
  46.1 0.3 fusion.11
  46.4 38.8 %all-gather.3.cloned.1.call-done = bf16[128,4,3072]{2,1,0:T(4,128)(2,1)} async-done(((bf16[1,4,3072]{2,1,0:T(4,128)(2,1)}), bf16[128,4,3072]{2,1,0:T(4,128)(2,1)}) %all-gather.3.cloned.1.call-update) | async-done | bytes 3145744 | tf_op jit(solution)/shard_map/all_gather | solution.py:9
  85.1 5.9 %reshape.42 = bf16[512,3072]{1,0:T(8,128)(2,1)} reshape(bf16[128,4,3072]{2,1,0:T(4,128)(2,1)} %all-gather.3.cloned.1.call-done) | data formatting | bytes 6291456
  91.1 0.0 copy-start.1
  91.1 6.5 %fusion.17 = (f32[512]{0:T(512)S(1)}, f32[512,1002]{0,1:T(8,128)S(1)}) fusion(bf16[512,3072]{1,0:T(8,128)(2,1)} %reshape.42, bf16[3072,1002]{0,1:T(8,128)(2,1)} %param.6), kind=kOutput, calls=%fused_computation.31 | convolution fusion | flops 3152531968 | bytes 11356160 | tf_op jit(solution)/shard_map/dot_general | solution.py:10
  97.6 62.3 %all-reduce.2 = (f32[512]{0:T(512)S(1)}, f32[512]{0:T(512)S(1)}) all-reduce(bf16[512]{0:T(512)(128)(2,1)S(1)} %fusion.11, f32[512]{0:T(512)S(1)} %get-tuple-element.13), channel_id=1, replica_groups=mesh['dp'=8,'vocab'=16] {'dp','vocab'}, use_global_device_ids=true, to_apply=%region_6.7 | all-reduce | flops 1024 | bytes 7168 | tf_op jit(solution)/shard_map/pmax | solution.py:23
  159.9 0.0 copy-done.1
  159.9 1.5 fusion.7
  161.4 64.1 %all-reduce.1 = (f32[512]{0:T(512)S(1)}, f32[512]{0:T(512)S(1)}, f32[512]{0:T(512)S(1)}, f32[512]{0:T(512)S(1)}) all-reduce(f32[512]{0:T(512)S(1)} %get-tuple-element.6, f32[512]{0:T(512)S(1)} %get-tuple-element.5, f32[512]{0:T(512)S(1)} %get-tuple-element.4, ...), channel_id=1, replica_groups=mesh['dp'=8,'vocab'=16] {'dp','vocab'}, use_global_device_ids=true, to_apply=%region_8.9 | all-reduce | flops 2048 | bytes 16384 | tf_op jit(solution)/shard_map/psum | solution.py:26
  225.5 9.5 %fusion.15 = f32[512,3072]{1,0:T(8,128)} fusion(bf16[3072,1002]{0,1:T(8,128)(2,1)} %param.6, f32[512,1002]{0,1:T(8,128)S(1)} %get-tuple-element.14, s32[512]{0:T(512)S(1)} %copy-done.1, f32[512]{0:T(512)S(1)} %get-tuple-element.7, f32[512]{0:T(512)S(1)} %get-tuple-element.11, f32[512]{0:T(512)S(1)} %get-tuple-element.8, f32[512]{0:T(512)S(1)} %get-tuple-element.12, ...), kind=kOutput, calls=%fused_computation.30 | convolution fusion | flops 3158688768 | bytes 15540648 | tf_op jit(solution)/shard_map/dot_general | solution.py:48
  235.1 0.0 all-reduce.5.cloned.1.call-update
  235.1 0.6 add_reduce_fusion
  236.4 9.2 %convolution_bitcast_fusion = f32[3072,1002]{0,1:T(8,128)} fusion(bf16[512,3072]{1,0:T(8,128)(2,1)} %reshape.42, f32[512,1002]{0,1:T(8,128)S(1)} %get-tuple-element.14, s32[512]{0:T(512)S(1)} %copy-done.1, f32[512]{0:T(512)S(1)} %get-tuple-element.7, f32[512]{0:T(512)S(1)} %get-tuple-element.11, f32[512]{0:T(512)S(1)} %get-tuple-element.8, ...), kind=kOutput, calls=%fused_computation.2 | convolution fusion | flops 3158688768 | bytes 18551208 | tf_op jit(solution)/shard_map/dot_general | solution.py:44
  245.5 144.3 %all-reduce.5.cloned.1.call-done = f32[512,3072]{1,0:T(8,128)} async-done(((f32[512,3072]{1,0:T(8,128)}), f32[512,3072]{1,0:T(8,128)}) %all-reduce.5.cloned.1.call-update) | async-done | bytes 6291472
  389.8 1.5 constant_dynamic-slice_fusion
  (6 shorter events, 0.0 us)
Async XLA Ops:
  7.2 78.0 %all-gather.3.cloned.1.call-start = ((), (), s32[]{:S(2)}) async-start(), calls=%async_computation.1 | async-start | bytes 3170304 | tf_op jit(solution)/shard_map/all_gather | solution.py:9
  10.9 13.4 %copy-start = (s32[512]{0:T(512)S(1)}, s32[512]{0:T(512)}, u32[]{:S(2)}) copy-start(s32[512]{0:T(512)} %param.8) | copy-start | bytes 6148
  12.7 30.3 %all-to-all-start = ((bf16[4,128,1002]{2,0,1:T(4,128)(2,1)}), bf16[4,128,1002]{2,0,1:T(4,128)(2,1)S(1)}, u32[]{:S(2)}, u32[]{:S(2)}) async-start(bf16[4,128,1002]{2,0,1:T(4,128)(2,1)} %copy.12), calls=%async_computation | async-start | bytes 2097152 | tf_op jit(solution)/shard_map/all_to_all | solution.py:15
  24.2 365.6 %all-reduce.5.cloned.1.call-start = ((), (), s32[]{:S(2)}) async-start(), calls=%async_computation.2 | async-start | bytes 12582912
  91.1 68.8 %copy-start.1 = (s32[512]{0:T(512)S(1)}, s32[512]{0:T(512)}, u32[]{:S(2)}) copy-start(s32[512]{0:T(512)} %param.9) | copy-start | bytes 6148
Sparse Core Ops, SparseCore 0:
  11.1 74.0 all-gather.2
  235.2 154.5 all-reduce.4
where the time goes:
time: 400 us; the launch traced here: 399 us
  waiting for transfers between devices  200 us (50%)
  blocking collectives  126 us (32%)
  matrix products  25.2 us (6%)
  local copies, waits for them, and re-layouts  17.7 us (4%)
  between operations  16 us (4%)
  starting transfers between devices  11.6 us (3%)
    unnamed x3, waiting for transfers between devices  145 us
    psum x1, blocking collectives, per_device(): lax.psum((jnp.sum(exp_student, axis=1), jnp.sum(exp_teacher, axis=1), jnp...  64.1 us
    pmax x1, blocking collectives, per_device(): lax.pmax((top_student, top_teacher), ('dp', 'vocab'))  62.3 us
    all_gather x1, waiting for transfers between devices, per_device(): gathered = lax.all_gather(hidden, ('dp', 'vocab'), axis=0, tiled=True)  38.8 us
    all_to_all x1, waiting for transfers between devices, per_device(): lax.all_to_all(teacher, ('dp', 'vocab'), split_axis=1, concat_axis=0, til...  16.2 us
    all_to_all x1, starting transfers between devices, per_device(): lax.all_to_all(teacher, ('dp', 'vocab'), split_axis=1, concat_axis=0, til...  11.5 us
    dot_general x1, matrix products, per_device(): lax.dot_general(dlogits, head_weight, (((1,), (1,)), ((), ())), preferred...  9.53 us
    dot_general x1, matrix products, per_device(): lax.dot_general(gathered, dlogits, (((0,), (0,)), ((), ())), preferred_el...  9.18 us
  transfers between devices with their start and end apart: 3, of which 3 were waited for; matrix products, arithmetic and copies ran while one was open for 4% of the time, Pallas kernels for 0%

commit v1 on v0

v1 whole, which is shorter than its diff:
```python
import jax
import jax.numpy as jnp
from jax import lax
from jax.experimental import pallas as pl
from jax.experimental.pallas import tpu as pltpu
from jax.sharding import Mesh, PartitionSpec as P

ALL = ("y", "core", "x", "z")
CHIPS = ("y", "x", "z")
SWAP = [(0, 1), (1, 0)]


def exchange(blocks, axes):
    return lax.all_to_all(blocks, axes, split_axis=0, concat_axis=0, tiled=True)


def spread(block, axes, count):
    return exchange(jnp.broadcast_to(block[None], (count,) + block.shape), axes)


def log_sum_exp(values, axis):
    top = jnp.max(values, axis=axis, keepdims=True)
    total = jnp.sum(jnp.exp(values - top), axis=axis)
    return jnp.squeeze(top, axis) + jnp.log(total)


def in_thirds(values):
    high = lax.reduce_precision(values, 8, 7)
    rest = values - high
    middle = lax.reduce_precision(rest, 8, 7)
    return jnp.stack([high, middle, rest - middle], axis=-1).astype(jnp.bfloat16)


def teach_kernel(offset_ref, token_ref, order_ref, label_ref, student_m_ref, student_o_ref,
                 loaded_ref, taught_m_ref, taught_o_ref, lse_ref, loss_ref):
    shard_width, half = student_m_ref.shape
    tokens = 2 * half
    pick = (token_ref[...] == order_ref[...]).astype(jnp.float32).astype(jnp.bfloat16)

    def columns(start, size):
        return lax.dot_general(
            loaded_ref[:, start : start + size],
            pick,
            (((0,), (0,)), ((), ())),
            preferred_element_type=jnp.float32,
        )

    last = shard_width // 128 * 128
    tail = columns(last, shard_width + 3 - last)
    row = lax.broadcasted_iota(jnp.int32, tail.shape, 0) + last
    lse = jnp.sum(jnp.where(row >= shard_width, tail, 0.0), axis=0, keepdims=True)
    lse_ref[...] = lse
    loss = jnp.zeros((1, tokens), jnp.float32)
    for start in range(0, shard_width, 128):
        size = min(128, shard_width - start)
        taught = tail[:size] if start == last else columns(start, size)
        at = pl.ds(start, size)
        taught_m_ref[at, :] = taught[:, :half].astype(jnp.bfloat16)
        taught_o_ref[at, :] = taught[:, half:].astype(jnp.bfloat16)
        student = jnp.concatenate([student_m_ref[at, :], student_o_ref[at, :]], axis=1)
        row = lax.broadcasted_iota(jnp.int32, (size, tokens), 0) + (start + offset_ref[0])
        term = jnp.exp(taught - lse) * (taught - student)
        term -= jnp.where(row == label_ref[...], 0.25 * student, 0.0)
        loss += jnp.sum(term, axis=0, keepdims=True)
    loss_ref[...] = sum(loss[:, k : k + 128] for k in range(0, tokens, 128))


def teach(offset, token, order, label, student_m, student_o, loaded):
    shard_width, half = student_m.shape
    tokens = 2 * half
    vmem = pl.BlockSpec(memory_space=pltpu.VMEM)
    return pl.pallas_call(
        teach_kernel,
        in_specs=[pl.BlockSpec(memory_space=pltpu.SMEM)] + [vmem] * 6,
        out_specs=[vmem] * 4,
        out_shape=[
            jax.ShapeDtypeStruct((shard_width, half), jnp.bfloat16),
            jax.ShapeDtypeStruct((shard_width, half), jnp.bfloat16),
            jax.ShapeDtypeStruct((1, tokens), jnp.float32),
            jax.ShapeDtypeStruct((1, 128), jnp.float32),
        ],
        compiler_params=pltpu.CompilerParams(vmem_limit_bytes=24 << 20),
        cost_estimate=pl.CostEstimate(
            flops=2 * shard_width * tokens * tokens,
            bytes_accessed=8 * shard_width * tokens,
            transcendentals=shard_width * tokens,
        ),
    )(offset, token, order, label, student_m, student_o, loaded)


def per_device(hidden, head_weight, teacher, row_token, labels):
    rows, width = hidden.shape
    shard_width = head_weight.shape[1]
    core = lax.axis_index("core")
    tokens = row_token.shape[0]
    half = tokens // 2
    devices = tokens // rows

    gathered = spread(hidden, CHIPS, devices // 2)

    lse_rows = in_thirds(log_sum_exp(teacher.astype(jnp.float32), 1))
    entries = teacher.reshape(rows, devices, shard_width).transpose(1, 0, 2)
    entries = jnp.concatenate(
        [entries, jnp.broadcast_to(lse_rows[None], (devices, rows, 3))], axis=2
    )
    loaded = exchange(entries, ALL)

    mine = gathered.reshape(half, width)
    other = lax.ppermute(mine, "core", SWAP)
    student_m = jnp.dot(mine, head_weight, preferred_element_type=jnp.float32)
    student_o = jnp.dot(other, head_weight, preferred_element_type=jnp.float32)
    lse_m, lse_o = log_sum_exp(student_m, 1), log_sum_exp(student_o, 1)
    loaded, student_m, student_o, lse_m, lse_o = lax.optimization_barrier(
        (loaded, student_m, student_o, lse_m, lse_o)
    )
    loaded = loaded.reshape(tokens, shard_width + 3)

    def flip(pair):
        return jnp.where(core == 0, pair, pair[::-1])

    def arranged(values):
        return flip(values.reshape(4, 2, half // 4).transpose(1, 0, 2).reshape(2, half))

    order = arranged(jnp.arange(tokens, dtype=jnp.int32))
    label_order = arranged(labels)
    first = lax.axis_index(ALL) * shard_width
    columns = first + lax.iota(jnp.int32, shard_width)
    taught_m, taught_o, lse_t, loss = teach(
        first[None],
        row_token[:, None],
        order.reshape(1, tokens),
        label_order.reshape(1, tokens),
        student_m.T,
        student_o.T,
        loaded,
    )

    stats = jnp.concatenate([flip(jnp.stack([lse_m, lse_o])).reshape(tokens), loss[0]])
    stats = spread(stats[None], ALL, devices).reshape(devices, tokens + 128)
    lse = log_sum_exp(stats[:, :tokens], 0)
    lse_t = lse_t.reshape(2, half)
    shift = flip(lse.reshape(2, half)), lse_t
    distill_loss = jnp.sum(stats[:, tokens:]) + jnp.sum(1.25 * lse.reshape(2, half) - flip(lse_t))
    distill_loss = distill_loss / tokens

    def gradient(index, student, taught):
        hit = label_order[index][:, None] == columns[None, :]
        return (
            80.0 * jnp.exp(student - shift[0][index][:, None])
            - 64.0 * jnp.exp(taught.T.astype(jnp.float32) - shift[1][index][:, None])
            - jnp.where(hit, 16.0, 0.0)
        ).astype(jnp.bfloat16)

    across = (((1,), (1,)), ((), ()))
    grad_o = gradient(1, student_o, taught_o)
    sent = lax.dot_general(grad_o, head_weight, across, preferred_element_type=jnp.float32)
    sent = sent.astype(jnp.bfloat16)
    received = lax.ppermute(sent, "core", SWAP)
    student_m, sent = lax.optimization_barrier((student_m, sent))
    grad_m = gradient(0, student_m, taught_m)
    kept = lax.dot_general(grad_m, head_weight, across, preferred_element_type=jnp.float32)
    kept, grad_m = lax.optimization_barrier((kept, grad_m))
    summed = (kept + received.astype(jnp.float32)).astype(jnp.bfloat16).reshape(devices // 2, rows, width)
    summed, grad_m, grad_o = lax.optimization_barrier((summed, grad_m, grad_o))
    pieces = exchange(summed, CHIPS)

    head_grad = lax.dot_general(
        jnp.concatenate([mine, other]),
        jnp.concatenate([grad_m, grad_o]),
        (((0,), (0,)), ((), ())),
        preferred_element_type=jnp.float32,
    )
    pieces, head_grad = lax.optimization_barrier((pieces, head_grad))
    hidden_grad = jnp.sum(pieces.astype(jnp.float32), axis=0)
    return (hidden_grad, head_grad, distill_loss)


def solution(mesh):
    grid = Mesh(mesh.devices.reshape(4, 2, 4, 4), ALL)
    in_specs = (P(ALL, None), P(None, ALL), P(ALL, None), P(), P())
    out_specs = (P(ALL, None), P(None, ALL), P())
    return jax.shard_map(
        per_device, mesh=grid, in_specs=in_specs, out_specs=out_specs, check_vma=False
    )
```

time: 400 us -> 129 us (0.32)
  waiting for transfers between devices: 200 us -> 42.2 us
  blocking collectives: 126 us -> 0 us
  starting transfers between devices: 11.6 us -> 31.3 us
  between operations: 16 us -> 3.42 us
  other arithmetic: 2.43 us -> 8.95 us
    unnamed x3 -> x0, waiting for transfers between devices: 145 us -> none
    psum x1 -> x0, blocking collectives: 64.1 us -> none  [per_device(): lax.psum((jnp.sum(exp_student, axis=1), jnp.sum(exp_teacher, axis=1), jnp...]
    pmax x1 -> x0, blocking collectives: 62.3 us -> none  [per_device(): lax.pmax((top_student, top_teacher), ('dp', 'vocab'))]
    all_gather x1 -> x0, waiting for transfers between devices: 38.8 us -> none  [per_device(): gathered = lax.all_gather(hidden, ('dp', 'vocab'), axis=0, tiled=True)]
    all_to_all x1 -> x4, waiting for transfers between devices: 16.2 us -> 41.5 us  [exchange(): return lax.all_to_all(blocks, axes, split_axis=0, concat_axis=0, tiled=True)]
    all_to_all x1 -> x4, starting transfers between devices: 11.5 us -> 28.8 us  [exchange(): return lax.all_to_all(blocks, axes, split_axis=0, concat_axis=0, tiled=True)]
    reshape x0 -> x8, local copies, waits for them, and re-layouts: none -> 7.41 us  [the longest x1 2.77 us: per_device(): entries = teacher.reshape(rows, devices, shard_width).transpose(1, 0, 2)]
    unnamed x6 -> x22, local copies, waits for them, and re-layouts: 7.48 us -> 1.63 us
  transfers between devices with their start and end apart: 3 -> 6, of which waited for: 3 -> 5; matrix products, arithmetic and copies ran while one was open for 4% -> 26% of each run, Pallas kernels for 0% -> 0%
where the time goes in v1:
time: 129 us; the launch traced here: 128 us
  waiting for transfers between devices  42.2 us (33%)
  starting transfers between devices  31.3 us (24%)
  matrix products  25.2 us (20%)
  local copies, waits for them, and re-layouts  15.3 us (12%)
  other arithmetic  8.95 us (7%)
  between operations  3.42 us (3%)
  Pallas kernels  1.31 us (1%)
    all_to_all x4, waiting for transfers between devices, exchange(): return lax.all_to_all(blocks, axes, split_axis=0, concat_axis=0, tiled=True)  41.5 us
    all_to_all x4, starting transfers between devices, exchange(): return lax.all_to_all(blocks, axes, split_axis=0, concat_axis=0, tiled=True)  28.8 us
    dot_general x1, matrix products, per_device(): lax.dot_general(jnp.concatenate([mine, other]), jnp.concatenate([grad_m,...  8.39 us
    dot_general x1, matrix products, per_device(): student_o = jnp.dot(other, head_weight, preferred_element_type=jnp.float32)  5.06 us
    dot_general x1, matrix products, per_device(): student_m = jnp.dot(mine, head_weight, preferred_element_type=jnp.float32)  5.06 us
    dot_general x1, matrix products, per_device(): lax.dot_general(grad_o, head_weight, across, preferred_element_type=jnp.f...  4.84 us
    broadcast_in_dim x2, local copies, waits for them, and re-layouts, spread(): return exchange(jnp.broadcast_to(block[None], (count,) + block.shape), axes)  3.26 us
    reshape x1, local copies, waits for them, and re-layouts, per_device(): entries = teacher.reshape(rows, devices, shard_width).transpose(1, 0, 2)  2.77 us
  transfers between devices with their start and end apart: 6, of which 5 were waited for; matrix products, arithmetic and copies ran while one was open for 26% of the time, Pallas kernels for 0%

profile of v1, /device:TPU:1, one launch (start us, length us, event | category | flops | bytes accessed | tf_op | source)
XLA Modules:
  0.0 127.7 jit_solution(5281049134577158950)
XLA Ops:
  0.6 2.4 %broadcast_in_dim.19 = bf16[64,4,3072]{2,1,0:T(4,128)(2,1)} broadcast(bf16[4,3072]{1,0:T(4,128)(2,1)} %param.5), dimensions={1,2} | broadcast | bytes 1597440 | tf_op jit(solution)/shard_map/broadcast_in_dim | solution.py:18
  3.0 12.0 %all-to-all-start.1 = ((bf16[64,4,3072]{2,1,0:T(4,128)(2,1)}), bf16[64,4,3072]{2,1,0:T(4,128)(2,1)S(1)}, u32[]{:S(2)}, u32[]{:S(2)}) async-start(bf16[64,4,3072]{2,1,0:T(4,128)(2,1)} %broadcast_in_dim.19), calls=%async_computation.1 | async-start | bytes 3145728 | tf_op jit(solution)/shard_map/all_to_all | solution.py:14
  15.0 2.8 %reshape.175 = bf16[4,128,1002]{2,1,0:T(8,128)(2,1)} reshape(bf16[4,128256]{1,0:T(4,128)(2,1)S(1)} %copy-done.4) | data formatting | bytes 2052096 | tf_op jit(solution)/shard_map/reshape | solution.py:102
  17.8 1.2 reduce_max.41
  19.0 1.2 exponential_reduce_fusion
  20.6 1.4 %pad_maximum_fusion = bf16[128,4,1005]{2,0,1:T(8,128)(2,1)S(1)} fusion(bf16[128,4,3]{2,0,1:T(8,128)(2,1)S(1)} %broadcast_in_dim.18, bf16[128,4,1002]{2,0,1:T(8,128)(2,1)} %bitcast.62), kind=kLoop, calls=%fused_computation.8 | loop fusion | flops 2058240 | bytes 2058240 | tf_op jit(solution)/shard_map/concatenate | solution.py:103
  22.0 1.8 %copy.26 = bf16[128,4,1005]{2,1,0:T(4,128)(2,1)} copy(bf16[128,4,1005]{2,0,1:T(8,128)(2,1)S(1)} %pad_maximum_fusion) | data formatting | bytes 2058240 | tf_op jit(solution)/shard_map/concatenate | solution.py:103
  23.8 13.7 %all-to-all-done.1 = bf16[64,4,3072]{2,1,0:T(4,128)(2,1)S(1)} async-done(((bf16[64,4,3072]{2,1,0:T(4,128)(2,1)}), bf16[64,4,3072]{2,1,0:T(4,128)(2,1)S(1)}, u32[]{:S(2)}, u32[]{:S(2)}) %all-to-all-start.1) | async-done | bytes 1572896 | tf_op jit(solution)/shard_map/all_to_all | solution.py:14
  37.5 7.1 %all-to-all-start = ((bf16[128,4,1005]{2,1,0:T(4,128)(2,1)}), bf16[128,4,1005]{2,1,0:T(4,128)(2,1)}, u32[]{:S(2)}, u32[]{:S(2)}) async-start(bf16[128,4,1005]{2,1,0:T(4,128)(2,1)} %copy.26), calls=%async_computation | async-start | bytes 2097152 | tf_op jit(solution)/shard_map/all_to_all | solution.py:14
  44.6 1.4 %reshape.176 = bf16[256,3072]{1,0:T(8,128)(2,1)} reshape(bf16[64,4,3072]{2,1,0:T(4,128)(2,1)S(1)} %all-to-all-done.1) | data formatting | bytes 3145728 | tf_op jit(solution)/shard_map/reshape | solution.py:108
  46.0 1.3 %collective-permute-start = (bf16[256,3072]{1,0:T(8,128)(2,1)}, bf16[256,3072]{1,0:T(8,128)(2,1)}, u32[]{:S(2)}, u32[]{:S(2)}) collective-permute-start(bf16[256,3072]{1,0:T(8,128)(2,1)} %reshape.176), channel_id=1, source_target_pairs={{0,16},{16,0},{1,17},{17,1},{2,18},{18,2},{3,19},{19,3},{4,20},{20... | collective-permute-start | bytes 4718600 | tf_op jit(solution)/shard_map/ppermute | solution.py:109
  47.7 5.1 %fusion.16 = (f32[256]{0:T(256)S(1)}, f32[256,1002]{0,1:T(8,128)S(1)}) fusion(bf16[256,3072]{1,0:T(8,128)(2,1)} %reshape.176, bf16[3072,1002]{0,1:T(8,128)(2,1)} %param.6), kind=kOutput, calls=%fused_computation.48 | convolution fusion | flops 1576265984 | bytes 8756224 | tf_op jit(solution)/shard_map/dot_general | solution.py:110
  53.0 5.1 %fusion.17 = (f32[256]{0:T(256)S(1)}, f32[256,1002]{0,1:T(8,128)S(1)}) fusion(bf16[256,3072]{1,0:T(8,128)(2,1)} %collective-permute-done, bf16[3072,1002]{0,1:T(8,128)(2,1)} %param.6), kind=kOutput, calls=%fused_computation.49 | convolution fusion | flops 1576265984 | bytes 8756224 | tf_op jit(solution)/shard_map/dot_general | solution.py:111
  58.3 4.7 %all-to-all-done = bf16[128,4,1005]{2,1,0:T(4,128)(2,1)} async-done(((bf16[128,4,1005]{2,1,0:T(4,128)(2,1)}), bf16[128,4,1005]{2,1,0:T(4,128)(2,1)}, u32[]{:S(2)}, u32[]{:S(2)}) %all-to-all-start) | async-done | bytes 1029152 | tf_op jit(solution)/shard_map/all_to_all | solution.py:14
  63.1 1.5 %reshape.189.loaded_ref = bf16[512,1005]{1,0:T(8,128)(2,1)S(1)} reshape(bf16[128,4,1005]{2,1,0:T(4,128)(2,1)} %all-to-all-done) | data formatting | bytes 2058240 | tf_op jit(solution)/shard_map/reshape | solution.py:116
  64.6 1.3 %shard_map.76 = (bf16[1002,256]{1,0:T(8,128)(2,1)S(1)}, bf16[1002,256]{1,0:T(8,128)(2,1)S(1)}, f32[1,512]{1,0:T(1,128)S(1)}, f32[1,128]{1,0:T(1,128)S(1)}) custom-call(s32[1]{0:T(128)} %bitcast.4.offset_ref, s32[512,1]{1,0:T(8,128)S(1)} %copy.28.token_ref, s32[1,512]{1,0:T(1,128)S(1)} %bitcast.57, s32[1,512]{1,0:T(1,128)S(1)} %bitcast.58, ...), custom_call_target="tpu_custom_call" | custom-call | flops 525336576 | bytes 4104192 | tf_op jit(solution)/shard_map/pallas_call | solution.py:72
  66.0 0.8 copy-done
  66.8 0.8 copy-done.2
  67.5 0.9 broadcast_in_dim.43
  68.4 4.9 %all-to-all-start.2 = ((f32[128,1,640]{2,1,0:T(1,128)}), f32[128,1,640]{2,1,0:T(1,128)S(1)}, u32[]{:S(2)}, u32[]{:S(2)}) async-start(f32[128,1,640]{2,1,0:T(1,128)} %broadcast_in_dim.43), calls=%async_computation.2 | async-start | bytes 655360 | tf_op jit(solution)/shard_map/all_to_all | solution.py:14
  73.9 0.7 reduce.4
  74.6 10.3 %all-to-all-done.2 = f32[128,1,640]{2,1,0:T(1,128)S(1)} async-done(((f32[128,1,640]{2,1,0:T(1,128)}), f32[128,1,640]{2,1,0:T(1,128)S(1)}, u32[]{:S(2)}, u32[]{:S(2)}) %all-to-all-start.2) | async-done | bytes 327712 | tf_op jit(solution)/shard_map/all_to_all | solution.py:14
  86.3 4.8 %convolution_convert_fusion = bf16[256,3072]{1,0:T(8,128)(2,1)S(1)} fusion(bf16[256,1002]{0,1:T(8,128)(2,1)S(1)} %fusion.10, bf16[3072,1002]{0,1:T(8,128)(2,1)} %param.6), kind=kOutput, calls=%fused_computation | convolution fusion | flops 1576796160 | bytes 8242176 | tf_op jit(solution)/shard_map/dot_general | solution.py:156
  91.2 1.2 collective-permute-start.1
  92.9 1.8 %fusion.18 = f32[256,3072]{1,0:T(8,128)S(1)} fusion(bf16[256,1002]{0,1:T(8,128)(2,1)S(1)} %fusion.8, bf16[3072,1002]{0,1:T(8,128)(2,1)S(1)} %bitcast.61), kind=kOutput, calls=%fused_computation.50 | convolution fusion | flops 1576009728 | bytes 9815040 | tf_op jit(solution)/shard_map/dot_general | solution.py:161
  94.7 0.7 collective-permute-done.1
  95.9 1.5 %reshape.191 = bf16[64,4,3072]{2,1,0:T(4,128)(2,1)} reshape(bf16[256,3072]{1,0:T(8,128)(2,1)S(1)} %add_convert_fusion) | data formatting | bytes 3145728 | tf_op jit(solution)/shard_map/reshape | solution.py:163
  97.3 4.9 %all-to-all-start.3 = ((bf16[64,4,3072]{2,1,0:T(4,128)(2,1)}), bf16[64,4,3072]{2,1,0:T(4,128)(2,1)S(1)}, u32[]{:S(2)}, u32[]{:S(2)}) async-start(bf16[64,4,3072]{2,1,0:T(4,128)(2,1)} %reshape.191), calls=%async_computation.3 | async-start | bytes 3145728 | tf_op jit(solution)/shard_map/all_to_all | solution.py:14
  102.2 0.6 slice_reduce_fusion.1
  104.2 8.4 %fusion = f32[3072,1002]{0,1:T(8,128)} fusion(bf16[256,3072]{1,0:T(8,128)(2,1)} %collective-permute-done, bf16[256,3072]{1,0:T(8,128)(2,1)} %reshape.176, bf16[256,1002]{0,1:T(8,128)(2,1)S(1)} %fusion.10, bf16[256,1002]{0,1:T(8,128)(2,1)S(1)} %fusion.8), kind=kOutput, calls=%fused_computation.1 | convolution fusion | flops 3160363008 | bytes 16484352 | tf_op jit(solution)/shard_map/dot_general | solution.py:167
  112.6 12.8 %all-to-all-done.3 = bf16[64,4,3072]{2,1,0:T(4,128)(2,1)S(1)} async-done(((bf16[64,4,3072]{2,1,0:T(4,128)(2,1)}), bf16[64,4,3072]{2,1,0:T(4,128)(2,1)S(1)}, u32[]{:S(2)}, u32[]{:S(2)}) %all-to-all-start.3) | async-done | bytes 1572896 | tf_op jit(solution)/shard_map/all_to_all | solution.py:14
  125.3 1.3 convert_reduce_fusion
  (64 shorter events, 4.2 us)
Async XLA Ops:
  0.6 14.4 %copy-start.4 = (bf16[4,128256]{1,0:T(4,128)(2,1)S(1)}, bf16[4,128256]{1,0:T(4,128)(2,1)}, u32[]{:S(2)}) copy-start(bf16[4,128256]{1,0:T(4,128)(2,1)} %param.7) | copy-start | bytes 3078148
  3.0 34.5 %all-to-all-start.1 = ((bf16[64,4,3072]{2,1,0:T(4,128)(2,1)}), bf16[64,4,3072]{2,1,0:T(4,128)(2,1)S(1)}, u32[]{:S(2)}, u32[]{:S(2)}) async-start(bf16[64,4,3072]{2,1,0:T(4,128)(2,1)} %broadcast_in_dim.19), calls=%async_computation.1 | async-start | bytes 3145728 | tf_op jit(solution)/shard_map/all_to_all | solution.py:14
  37.5 25.5 %all-to-all-start = ((bf16[128,4,1005]{2,1,0:T(4,128)(2,1)}), bf16[128,4,1005]{2,1,0:T(4,128)(2,1)}, u32[]{:S(2)}, u32[]{:S(2)}) async-start(bf16[128,4,1005]{2,1,0:T(4,128)(2,1)} %copy.26), calls=%async_computation | async-start | bytes 2097152 | tf_op jit(solution)/shard_map/all_to_all | solution.py:14
  44.6 2.7 %copy-start.6 = (s32[512]{0:T(512)S(1)}, s32[512]{0:T(512)}, u32[]{:S(2)}) copy-start(s32[512]{0:T(512)} %param.9) | copy-start | bytes 6148
  44.6 2.9 %copy-start.5 = (s32[512]{0:T(512)S(1)}, s32[512]{0:T(512)}, u32[]{:S(2)}) copy-start(s32[512]{0:T(512)} %param.8) | copy-start | bytes 6148
  46.0 7.0 %collective-permute-start = (bf16[256,3072]{1,0:T(8,128)(2,1)}, bf16[256,3072]{1,0:T(8,128)(2,1)}, u32[]{:S(2)}, u32[]{:S(2)}) collective-permute-start(bf16[256,3072]{1,0:T(8,128)(2,1)} %reshape.176), channel_id=1, source_target_pairs={{0,16},{16,0},{1,17},{17,1},{2,18},{18,2},{3,19},{19,3},{4,20},{20... | collective-permute-start | bytes 4718600 | tf_op jit(solution)/shard_map/ppermute | solution.py:109
  66.0 0.8 copy-start
  66.8 0.8 copy-start.2
  67.5 18.3 %copy-start.3 = (bf16[1002,256]{1,0:T(8,128)(2,1)S(1)}, bf16[1002,256]{1,0:T(8,128)(2,1)}, u32[]{:S(2)}) copy-start(bf16[1002,256]{1,0:T(8,128)(2,1)} %copy-done.2) | copy-start | bytes 1539076
  68.4 16.5 %all-to-all-start.2 = ((f32[128,1,640]{2,1,0:T(1,128)}), f32[128,1,640]{2,1,0:T(1,128)S(1)}, u32[]{:S(2)}, u32[]{:S(2)}) async-start(f32[128,1,640]{2,1,0:T(1,128)} %broadcast_in_dim.43), calls=%async_computation.2 | async-start | bytes 655360 | tf_op jit(solution)/shard_map/all_to_all | solution.py:14
  85.8 7.0 %slice-start = ((s8[6193152]{0:T(1024)(128)(4,1)}), s8[4194304]{0:T(1024)(128)(4,1)S(1)}, s32[]{:S(2)}) async-start(s8[6193152]{0:T(1024)(128)(4,1)} %bitcast.60), calls=%async_computation.4 | async-start | bytes 8388608
  86.3 6.1 %copy-start.1 = (bf16[1002,256]{1,0:T(8,128)(2,1)S(1)}, bf16[1002,256]{1,0:T(8,128)(2,1)}, u32[]{:S(2)}) copy-start(bf16[1002,256]{1,0:T(8,128)(2,1)} %copy-done) | copy-start | bytes 1539076
  86.3 6.6 %slice-start.1 = ((s8[6193152]{0:T(1024)(128)(4,1)}), s8[1998848]{0:T(1024)(128)(4,1)S(1)}, s32[]{:S(2)}) async-start(s8[6193152]{0:T(1024)(128)(4,1)} %bitcast.60), calls=%async_computation.5 | async-start | bytes 3997696
  91.2 4.3 %collective-permute-start.1 = (bf16[256,3072]{1,0:T(8,128)(2,1)S(1)}, bf16[256,3072]{1,0:T(8,128)(2,1)S(1)}, u32[]{:S(2)}, u32[]{:S(2)}) collective-permute-start(bf16[256,3072]{1,0:T(8,128)(2,1)S(1)} %convolution_convert_fusion), channel_id=1, source_target_pairs={{0,16},{16,0},{1,17},{17,1},{2,18},{18,2},{3,19},{19,3},{4,20},{20... | collective-permute-start | bytes 4718600 | tf_op jit(solution)/shard_map/ppermute | solution.py:158
  97.3 28.0 %all-to-all-start.3 = ((bf16[64,4,3072]{2,1,0:T(4,128)(2,1)}), bf16[64,4,3072]{2,1,0:T(4,128)(2,1)S(1)}, u32[]{:S(2)}, u32[]{:S(2)}) async-start(bf16[64,4,3072]{2,1,0:T(4,128)(2,1)} %reshape.191), calls=%async_computation.3 | async-start | bytes 3145728 | tf_op jit(solution)/shard_map/all_to_all | solution.py:14
